TPU v7x, 128 devices: a whole 4x4x4 slice. The times are simulated.
128 devices in a mesh: patch: 16 (over x, y_hi, core), head: 8 (over y_lo, z).
Axes of the slice: x: 4, y: 4 (y_hi: 2, y_lo: 2; y = y_hi * 2 + y_lo), z: 4, core: 2. Of those that a mesh axis runs over, the one named last changes fastest.
Arguments:
- image_query: bfloat16 [16384, 2048], P(('patch', 'head')), may hold values from -120 to 120
- image_key: bfloat16 [16384, 2048], P(('patch', 'head')), may hold values from -6 to 6
- image_value: bfloat16 [16384, 2048], P(('patch', 'head')), may hold values from -6 to 6
- positions: int32 [3, 16384], P(None, ('patch', 'head')), may hold values from 0 to 63
- stale_key: bfloat16 [16384, 2048], P('patch', 'head'), may hold values from -6 to 6
- stale_value: bfloat16 [16384, 2048], P('patch', 'head'), may hold values from -6 to 6
- text_query: bfloat16 [256, 2048], P(None, 'head'), may hold values from -120 to 120
- text_key: bfloat16 [256, 2048], P(None, 'head'), may hold values from -6 to 6
- text_value: bfloat16 [256, 2048], P(None, 'head'), may hold values from -6 to 6
- text_len: int32 [1], replicated, may hold values from 64 to 256
Outputs:
- image_out: bfloat16 [16384, 2048], P(('patch', 'head'))
- text_out: bfloat16 [256, 2048], P(None, 'head')
All inputs are finite; a program needn't handle non-finite values.
Results may differ from a plain program's by a relative error of at most 0.0086.
Values may be sent and summed in bfloat16 or wider, within the bound.
A program may use at most 128 MiB of HBM per device.

v0:
```python
import jax
import jax.numpy as jnp
import numpy as np
from jax import lax
from jax.sharding import PartitionSpec as P

HD = 128


THETA = 256.0


def joined(value, axis, join):
    pieces = jax.tree.map(lambda part: lax.all_gather(part, axis), value)
    head = jax.tree.map(lambda part: part[0], pieces)
    tail = jax.tree.map(lambda part: part[1:], pieces)
    total, _ = lax.scan(lambda total, section: (join(total, section), None), head, tail)
    return total


def pair_tables(head_dim):
    first = head_dim // 8
    second = (head_dim - first) // 2
    parts = [first, second, head_dim - first - second]
    freqs = []
    which = []
    for axis_id in range(3):
        width = parts[axis_id]
        for index in range(width // 2):
            freqs.append(THETA ** (-2.0 * index / width))
            which.append(axis_id)
    return (np.array(freqs, dtype=np.float32), np.array(which, dtype=np.int32), parts)


def rotate(values, positions):
    freqs, which, parts = pair_tables(HD)
    count = values.shape[0]
    pos = positions.astype(jnp.float32)
    angles = jnp.take(pos, jnp.asarray(which), axis=0).T * jnp.asarray(freqs)[None, :]
    cosine = jnp.cos(angles)[:, None, :]
    sine = jnp.sin(angles)[:, None, :]
    heads = values.astype(jnp.float32).reshape(count, -1, HD)
    pieces = []
    begin = 0
    pair_start = 0
    for width in parts:
        half = width // 2
        low = heads[:, :, begin : begin + half]
        high = heads[:, :, begin + half : begin + width]
        c = cosine[:, :, pair_start : pair_start + half]
        s = sine[:, :, pair_start : pair_start + half]
        pieces.append(low * c - high * s)
        pieces.append(low * s + high * c)
        begin = begin + width
        pair_start = pair_start + half
    return jnp.concatenate(pieces, axis=2).reshape(count, -1).astype(jnp.bfloat16)


def heads_view(values):
    return values.reshape(values.shape[0], -1, HD)


def empty_state(local_heads, rows):
    return (
        jnp.full((local_heads, rows), -jnp.inf, jnp.float32),
        jnp.zeros((local_heads, rows), jnp.float32),
        jnp.zeros((local_heads, rows, HD), jnp.float32),
    )


def fold_block(state, queries, keys, values, valid):
    top_old, total, acc = state
    scores = jnp.einsum("qhd,khd->hqk", queries, keys, preferred_element_type=jnp.float32) * HD ** (
        -0.5
    )
    scores = jnp.where(valid[None, None, :], scores, -jnp.inf)
    top = jnp.maximum(top_old, jnp.max(scores, axis=2))
    keep = jnp.exp(top_old - top)
    weights = jnp.exp(scores - top[:, :, None])
    total = total * keep + jnp.sum(weights, axis=2)
    acc = acc * keep[:, :, None] + jnp.einsum(
        "hqk,khd->hqd", weights.astype(jnp.bfloat16), values, preferred_element_type=jnp.float32
    )
    return (top, total, acc)


def combine_states(first, second):
    top = jnp.maximum(first[0], second[0])
    left = jnp.exp(first[0] - top)
    right = jnp.exp(second[0] - top)
    return (
        top,
        first[1] * left + second[1] * right,
        first[2] * left[:, :, None] + second[2] * right[:, :, None],
    )


def finish(state):
    mixed = state[2] / state[1][:, :, None]
    return mixed.transpose(1, 0, 2).reshape(mixed.shape[1], -1).astype(jnp.bfloat16)


def body(
    image_query,
    image_key,
    image_value,
    positions,
    stale_key,
    stale_value,
    text_query,
    text_key,
    text_value,
    text_len,
):
    rotated_query = rotate(image_query, positions)
    rotated_key = rotate(image_key, positions)
    fresh_query, fresh_key, fresh_value = (
        lax.all_to_all(rotated_query, "head", split_axis=1, concat_axis=0, tiled=True),
        lax.all_to_all(rotated_key, "head", split_axis=1, concat_axis=0, tiled=True),
        lax.all_to_all(image_value, "head", split_axis=1, concat_axis=0, tiled=True),
    )
    rows = fresh_query.shape[0]
    local_heads = stale_key.shape[1] // HD
    patch_index = lax.axis_index("patch")
    own_start = patch_index * rows
    text_valid = jnp.arange(text_key.shape[0]) < text_len[0]
    query_heads = heads_view(fresh_query)
    key_heads = heads_view(fresh_key)
    value_heads = heads_view(fresh_value)
    text_keys = heads_view(text_key)
    text_values = heads_view(text_value)
    all_rows = jnp.ones((rows,), bool)
    state = empty_state(local_heads, rows)
    state = fold_block(state, query_heads, key_heads, value_heads, all_rows)
    state = fold_block(state, query_heads, text_keys, text_values, text_valid)

    def stale_block(carry, keys, values, start):
        index = start + jnp.arange(keys.shape[0])
        valid = (index < own_start) | (index >= own_start + rows)
        return fold_block(carry, query_heads, heads_view(keys), heads_view(values), valid)

    gathered_key, gathered_value = (
        lax.all_gather(stale_key, "patch", axis=0, tiled=True),
        lax.all_gather(stale_value, "patch", axis=0, tiled=True),
    )
    length = gathered_key.shape[0]
    block = min(rows, length)
    count = length // block

    def step(index, inner):
        offset = index * block
        keys = lax.dynamic_slice_in_dim(gathered_key, offset, block, 0)
        values = lax.dynamic_slice_in_dim(gathered_value, offset, block, 0)
        return stale_block(inner, keys, values, offset)

    state = lax.fori_loop(0, count, step, state)
    image_out = lax.all_to_all(finish(state), "head", split_axis=0, concat_axis=1, tiled=True)
    text_heads = heads_view(text_query)
    text_state = empty_state(local_heads, text_query.shape[0])
    text_state = fold_block(text_state, text_heads, key_heads, value_heads, all_rows)
    text_state = fold_block(
        text_state, text_heads, text_keys, text_values, text_valid & (patch_index == 0)
    )
    text_state = joined(text_state, "patch", combine_states)
    return (image_out, finish(text_state))


def solution(mesh):
    return jax.shard_map(
        body,
        mesh=mesh,
        in_specs=(
            P(("patch", "head"), None),
            P(("patch", "head"), None),
            P(("patch", "head"), None),
            P(None, ("patch", "head")),
            P("patch", "head"),
            P("patch", "head"),
            P(None, "head"),
            P(None, "head"),
            P(None, "head"),
            P(),
        ),
        out_specs=(P(("patch", "head"), None), P(None, "head")),
        check_vma=False,
    )
```

profile of v0, /device:TPU:1, one launch (start us, length us, event | category | flops | bytes accessed | tf_op | source)
XLA Modules:
  0.0 431.1 jit_solution(439172601130657789)
XLA Ops:
  13.5 5.7 %concatenate.9 = bf16[128,16,128]{0,2,1:T(8,128)(2,1)} concatenate(bf16[128,16,8]{0,2,1:T(8,128)(2,1)S(1)} %get-tuple-element.308, bf16[128,16,8]{0,2,1:T(8,128)(2,1)S(1)} %get-tuple-element.307, bf16[128,16,28]{0,2,1:T(8,128)(2,1)S(1)} %get-tuple-element.311, bf16[128,16,28]{0,2,1:T(8,128)(2,1)S(1)} %get-tuple-element.312, bf16[128,16,28]{0,2,1:T(8,128)(2,1)S(1)} %get-tuple-element.300, ...), dimensions={2} | concatenate | bytes 1048576 | tf_op jit(solution)/shard_map/concatenate | solution.py:56
  19.2 6.9 %all-to-all-start.1 = ((bf16[128,8,256]{0,2,1:T(8,128)(2,1)}), bf16[128,8,256]{0,2,1:T(8,128)(2,1)S(1)}, u32[]{:S(2)}, u32[]{:S(2)}) async-start(bf16[128,8,256]{0,2,1:T(8,128)(2,1)} %bitcast.22), calls=%async_computation.1 | async-start | bytes 1048576 | tf_op jit(solution)/shard_map/all_to_all | solution.py:119
  27.7 6.1 %all-to-all-done.1 = bf16[128,8,256]{0,2,1:T(8,128)(2,1)S(1)} async-done(((bf16[128,8,256]{0,2,1:T(8,128)(2,1)}), bf16[128,8,256]{0,2,1:T(8,128)(2,1)S(1)}, u32[]{:S(2)}, u32[]{:S(2)}) %all-to-all-start.1) | async-done | bytes 524320 | tf_op jit(solution)/shard_map/all_to_all | solution.py:119
  33.8 5.2 %all-to-all-start.2 = ((bf16[128,8,256]{0,2,1:T(8,128)(2,1)}), bf16[128,8,256]{0,2,1:T(8,128)(2,1)}, u32[]{:S(2)}, u32[]{:S(2)}) async-start(bf16[128,8,256]{0,2,1:T(8,128)(2,1)} %bitcast.25), calls=%async_computation.2 | async-start | bytes 1048576 | tf_op jit(solution)/shard_map/all_to_all | solution.py:120
  61.0 9.1 %concatenate.8 = bf16[128,16,128]{0,2,1:T(8,128)(2,1)} concatenate(bf16[128,16,8]{0,2,1:T(8,128)(2,1)} %get-tuple-element.322, bf16[128,16,8]{0,2,1:T(8,128)(2,1)} %get-tuple-element.323, bf16[128,16,28]{0,2,1:T(8,128)(2,1)} %get-tuple-element.313, bf16[128,16,28]{0,2,1:T(8,128)(2,1)} %get-tuple-element.314, bf16[128,16,28]{0,2,1:T(8,128)(2,1)} %get-tuple-element.304, ...), dimensions={2} | concatenate | bytes 1048576 | tf_op jit(solution)/shard_map/concatenate | solution.py:56
  70.1 5.1 %all-to-all-start = ((bf16[128,8,256]{0,2,1:T(8,128)(2,1)}), bf16[128,8,256]{0,2,1:T(8,128)(2,1)S(1)}, u32[]{:S(2)}, u32[]{:S(2)}) async-start(bf16[128,8,256]{0,2,1:T(8,128)(2,1)} %bitcast.19), calls=%async_computation | async-start | bytes 1048576 | tf_op jit(solution)/shard_map/all_to_all | solution.py:118
  78.2 26.1 %all_gather.22 = f32[16,2,256]{2,1,0:T(2,128)S(1)} all-gather(f32[1,2,256]{2,1,0:T(2,128)S(1)} %get-tuple-element.325), channel_id=1, replica_groups=mesh['patch'=16,'head'=8] {'patch'}, dimensions={0}, use_global_device_ids=true | all-gather | bytes 34816 | tf_op jit(solution)/shard_map/all_gather | solution.py:14
  104.3 19.3 %all_gather.23 = f32[16,2,256]{2,1,0:T(2,128)S(1)} all-gather(f32[1,2,256]{2,1,0:T(2,128)S(1)} %get-tuple-element.324), channel_id=1, replica_groups=mesh['patch'=16,'head'=8] {'patch'}, dimensions={0}, use_global_device_ids=true | all-gather | bytes 34816 | tf_op jit(solution)/shard_map/all_gather | solution.py:14
  131.6 4.4 %slice.147 = f32[30,256,128]{2,1,0:T(8,128)} slice(f32[32,256,128]{2,1,0:T(8,128)} %all-gather.9.cloned.1.call-done), slice={[2:32], [0:256], [0:128]} | slice | bytes 7864320 | tf_op jit(solution)/shard_map/slice | solution.py:16
  136.0 51.7 %all-gather.5.cloned.1.call-done = bf16[16384,256]{0,1:T(8,128)(2,1)} async-done(((bf16[1024,256]{0,1:T(8,128)(2,1)}), bf16[16384,256]{0,1:T(8,128)(2,1)}) %all-gather.5.cloned.1.call-update) | async-done | bytes 8388624 | tf_op jit(solution)/shard_map/all_gather | solution.py:143
  187.7 73.1 %all-gather.7.cloned.1.call-done = bf16[16384,256]{0,1:T(8,128)(2,1)} async-done(((bf16[1024,256]{0,1:T(8,128)(2,1)}), bf16[16384,256]{0,1:T(8,128)(2,1)}) %all-gather.7.cloned.1.call-update) | async-done | bytes 8388624 | tf_op jit(solution)/shard_map/all_gather | solution.py:144
  260.8 137.4 %while.32 = (s32[]{:T(128)}, f32[2,1024]{1,0:T(2,128)S(1)}, f32[2,1024]{1,0:T(2,128)S(1)}, f32[2,1024,128]{2,1,0:T(8,128)S(1)}, s32[]{:T(128)}, /*index=5*/s32[]...) while((s32[]{:T(128)}, f32[2,1024]{1,0:T(2,128)S(1)}, ...), condition=%wide.region_7.9_spmd, body=%wide.region_4.8_spmd.sunk | while | flops 1097342976 | bytes 31068348 | solution.py:156
  266.7 2.7 fusion.106
  275.3 2.7 fusion.106
  283.9 2.7 fusion.106
  292.4 2.7 fusion.106
  309.6 2.7 fusion.106
  335.4 2.7 fusion.106
  344.0 2.7 fusion.106
  361.2 2.7 fusion.106
  369.8 2.7 fusion.106
  395.5 2.7 fusion.106
  399.8 4.2 all-to-all-start.3
  404.0 18.8 %while.33 = (s32[]{:T(128)}, f32[2,256]{1,0:T(2,128)S(1)}, f32[2,256]{1,0:T(2,128)S(1)}, f32[2,256,128]{2,1,0:T(8,128)S(1)}, f32[15,2,256]{2,1,0:T(2,128)S(1)}, ...) while((s32[]{:T(128)}, f32[2,256]{1,0:T(2,128)S(1)}, f32[2,256]{1,0:T(2,128)S(1)}, ...), condition=%wide.region_13.15_spmd, body=%wide.region_12.14_spmd.sunk | while | flops 199682 | bytes 807005 | solution.py:17
  (237 shorter events, 171.7 us)
Async XLA Ops:
  7.2 31.9 %copy-start = (bf16[256,256]{1,0:T(8,128)(2,1)S(1)}, bf16[256,256]{1,0:T(8,128)(2,1)}, u32[]{:S(2)}) copy-start(bf16[256,256]{1,0:T(8,128)(2,1)} %param.27) | copy-start | bytes 393220
  7.2 19.5 %copy-start.5 = (bf16[128,2048]{1,0:T(8,128)(2,1)S(1)}, bf16[128,2048]{1,0:T(8,128)(2,1)}, u32[]{:S(2)}) copy-start(bf16[128,2048]{1,0:T(8,128)(2,1)} %param.22) | copy-start | bytes 1572868
  10.1 17.6 %copy-start.6 = (f32[128,28]{0,1:T(8,128)}, f32[128,28]{0,1:T(8,128)S(1)}, u32[]{:S(2)}) copy-start(f32[128,28]{0,1:T(8,128)S(1)} %get-tuple-element.320) | copy-start | bytes 43012
  10.1 17.6 %copy-start.7 = (f32[128,28]{0,1:T(8,128)}, f32[128,28]{0,1:T(8,128)S(1)}, u32[]{:S(2)}) copy-start(f32[128,28]{0,1:T(8,128)S(1)} %get-tuple-element.335) | copy-start | bytes 43012
  10.1 17.6 %copy-start.8 = (f32[128,28]{0,1:T(8,128)}, f32[128,28]{0,1:T(8,128)S(1)}, u32[]{:S(2)}) copy-start(f32[128,28]{0,1:T(8,128)S(1)} %get-tuple-element.336) | copy-start | bytes 43012
  11.4 27.7 %copy-start.9 = (bf16[256,256]{1,0:T(8,128)(2,1)S(1)}, bf16[256,256]{1,0:T(8,128)(2,1)}, u32[]{:S(2)}) copy-start(bf16[256,256]{1,0:T(8,128)(2,1)} %param.26) | copy-start | bytes 393220
  19.2 14.7 %all-to-all-start.1 = ((bf16[128,8,256]{0,2,1:T(8,128)(2,1)}), bf16[128,8,256]{0,2,1:T(8,128)(2,1)S(1)}, u32[]{:S(2)}, u32[]{:S(2)}) async-start(bf16[128,8,256]{0,2,1:T(8,128)(2,1)} %bitcast.22), calls=%async_computation.1 | async-start | bytes 1048576 | tf_op jit(solution)/shard_map/all_to_all | solution.py:119
  33.8 12.5 %all-to-all-start.2 = ((bf16[128,8,256]{0,2,1:T(8,128)(2,1)}), bf16[128,8,256]{0,2,1:T(8,128)(2,1)}, u32[]{:S(2)}, u32[]{:S(2)}) async-start(bf16[128,8,256]{0,2,1:T(8,128)(2,1)} %bitcast.25), calls=%async_computation.2 | async-start | bytes 1048576 | tf_op jit(solution)/shard_map/all_to_all | solution.py:120
  39.0 92.6 %all-gather.9.cloned.1.call-start = ((), (), s32[]{:S(2)}) async-start(), calls=%async_computation.6 | async-start | bytes 4456448 | tf_op jit(solution)/shard_map/all_gather | solution.py:14
  41.1 11.9 %copy-start.4 = (bf16[256,256]{1,0:T(8,128)(2,1)S(1)}, bf16[256,256]{1,0:T(8,128)(2,1)}, u32[]{:S(2)}) copy-start(bf16[256,256]{1,0:T(8,128)(2,1)} %param.28) | copy-start | bytes 393220
  51.3 8.0 %copy-start.12 = (f32[2,256]{1,0:T(2,128)}, f32[2,256]{1,0:T(2,128)S(1)}, u32[]{:S(2)}) copy-start(f32[2,256]{1,0:T(2,128)S(1)} %get-tuple-element.292) | copy-start | bytes 6148
  55.0 132.7 %all-gather.5.cloned.1.call-start = ((), (), s32[]{:S(2)}) async-start(), calls=%async_computation.4 | async-start | bytes 8912896 | tf_op jit(solution)/shard_map/all_gather | solution.py:143
  57.2 203.6 %all-gather.7.cloned.1.call-start = ((), (), s32[]{:S(2)}) async-start(), calls=%async_computation.5 | async-start | bytes 8912896 | tf_op jit(solution)/shard_map/all_gather | solution.py:144
  70.1 53.6 %all-to-all-start = ((bf16[128,8,256]{0,2,1:T(8,128)(2,1)}), bf16[128,8,256]{0,2,1:T(8,128)(2,1)S(1)}, u32[]{:S(2)}, u32[]{:S(2)}) async-start(bf16[128,8,256]{0,2,1:T(8,128)(2,1)} %bitcast.19), calls=%async_computation | async-start | bytes 1048576 | tf_op jit(solution)/shard_map/all_to_all | solution.py:118
  76.3 48.7 %copy-start.3 = (bf16[1024,2,128]{0,2,1:T(8,128)(2,1)S(1)}, bf16[1024,2,128]{0,2,1:T(8,128)(2,1)}, u32[]{:S(2)}) copy-start(bf16[1024,2,128]{0,2,1:T(8,128)(2,1)} %reshape.191) | copy-start | bytes 1572868
  104.3 22.0 %copy-start.10 = (f32[16,2,256]{2,1,0:T(2,128)}, f32[16,2,256]{2,1,0:T(2,128)S(1)}, u32[]{:S(2)}) copy-start(f32[16,2,256]{2,1,0:T(2,128)S(1)} %all_gather.22) | copy-start | bytes 98308
  123.6 2.6 copy-start.11
  126.8 1.4 copy-start.2
  398.2 5.8 %slice-start = ((f32[32,256,128]{2,1,0:T(8,128)}), f32[2,256,128]{2,1,0:T(8,128)S(1)}, s32[]{:S(2)}) async-start(f32[32,256,128]{2,1,0:T(8,128)} %all-gather.9.cloned.1.call-done), calls=%async_computation.7 | async-start | bytes 524288 | tf_op jit(solution)/shard_map/slice | solution.py:15
  398.2 5.8 %slice-start.1 = ((f32[16,2,256]{2,1,0:T(2,128)}), f32[15,2,256]{2,1,0:T(2,128)S(1)}, s32[]{:S(2)}) async-start(f32[16,2,256]{2,1,0:T(2,128)} %copy-done.10), calls=%async_computation.8 | async-start | bytes 61440 | tf_op jit(solution)/shard_map/slice | solution.py:16
  398.2 5.8 %slice-start.2 = ((f32[16,2,256]{2,1,0:T(2,128)}), f32[15,2,256]{2,1,0:T(2,128)S(1)}, s32[]{:S(2)}) async-start(f32[16,2,256]{2,1,0:T(2,128)} %copy-done.11), calls=%async_computation.9 | async-start | bytes 61440 | tf_op jit(solution)/shard_map/slice | solution.py:16
  398.8 25.8 %copy-start.1 = (bf16[256,256]{1,0:T(8,128)(2,1)S(1)}, bf16[256,256]{1,0:T(8,128)(2,1)}, u32[]{:S(2)}) copy-start(bf16[256,256]{1,0:T(8,128)(2,1)} %param.27) | copy-start | bytes 393220
  399.8 23.8 %all-to-all-start.3 = ((bf16[8,128,256]{1,2,0:T(8,128)(2,1)}), bf16[8,128,256]{1,2,0:T(8,128)(2,1)S(1)}, u32[]{:S(2)}, u32[]{:S(2)}) async-start(bf16[8,128,256]{1,2,0:T(8,128)(2,1)} %copy.117), calls=%async_computation.3 | async-start | bytes 1048576 | tf_op jit(solution)/shard_map/all_to_all | solution.py:157
Sparse Core Ops, SparseCore 0:
  55.1 58.5 all-gather.8
  116.2 71.5 all-gather.4
  190.2 70.5 all-gather.6
where the time goes:
time: 433 us; the launch traced here: 431 us
  waiting for transfers between devices  133 us (31%)
  matrix products  90.1 us (21%)
  other arithmetic  68.4 us (16%)
  local copies, waits for them, and re-layouts  56.7 us (13%)
  blocking collectives  45.4 us (10%)
  starting transfers between devices  21.4 us (5%)
  between operations  14.8 us (3%)
    all_gather x1, waiting for transfers between devices, body(): lax.all_gather(stale_value, 'patch', axis=0, tiled=True)  73.1 us
    all_gather x1, waiting for transfers between devices, body(): lax.all_gather(stale_key, 'patch', axis=0, tiled=True)  51.7 us
    dot_general x20, matrix products, fold_block(): jnp.einsum('hqk,khd->hqd', weights.astype(jnp.bfloat16), values, preferre...  49.5 us
    all_gather x2, blocking collectives, joined(): pieces = jax.tree.map(lambda part: lax.all_gather(part, axis), value)  45.4 us
    reduce_sum x20, other arithmetic, fold_block(): total = total * keep + jnp.sum(weights, axis=2)  41.9 us
    dot_general x20, matrix products, fold_block(): jnp.einsum('qhd,khd->hqk', queries, keys, preferred_element_type=jnp.floa...  40.6 us
    dynamic_slice x16, local copies, waits for them, and re-layouts, step(): values = lax.dynamic_slice_in_dim(gathered_value, offset, block, 0)  20.4 us
    add x15, other arithmetic, combine_states(): first[2] * left[:, :, None] + second[2] * right[:, :, None]  18.1 us
  transfers between devices with their start and end apart: 7, of which 4 were waited for; matrix products, arithmetic and copies ran while one was open for 13% of the time, Pallas kernels for 0%

commit v1 on v0

v1 whole, which is shorter than its diff:
```python
import functools

import jax
import jax.numpy as jnp
import numpy as np
from jax import lax
from jax.experimental import pallas as pl
from jax.experimental.pallas import tpu as pltpu
from jax.sharding import PartitionSpec as P

HD = 128
THETA = 256.0
MESH = pl.DeviceIdType.MESH
SCALE = 1.4426950408889634 * HD ** (-0.5)
LOW = -1e30
TILE = 1024
PIECE = 512
BLOCK = 128
TXT = 256

NEAR_A, NEAR_B, FAR, OWN = (4, 6, 8, 10), (5, 7, 9, 11), (12, 13, 14, 15), (0, 1, 2, 3)
ITEMS = [
    (0, NEAR_A), (1, NEAR_A),
    (0, (16, 17, 2, 3)), (1, (0, 1, 18, 19)),
    (0, NEAR_B), (1, NEAR_B),
    (2, OWN), (3, OWN),
    (2, NEAR_A), (3, NEAR_A),
    (2, NEAR_B), (3, NEAR_B),
    (2, FAR), (3, FAR),
    (0, FAR), (1, FAR),
]


def rotation_tables():
    first = HD // 8
    second = (HD - first) // 2
    freqs = np.zeros((HD,), np.float32)
    which = np.zeros((HD,), np.int32)
    swap = np.zeros((HD, HD), np.float32)
    begin = 0
    for axis_id, width in enumerate([first, second, HD - first - second]):
        half = width // 2
        for index in range(half):
            low, high = begin + index, begin + index + half
            freqs[low] = freqs[high] = np.float32(THETA ** (-2.0 * index / width))
            which[low] = which[high] = axis_id
            swap[high, low] = -1.0
            swap[low, high] = 1.0
        begin += width
    return freqs, which, swap


def pick(i, values):
    out = values[0]
    for j in range(1, len(values)):
        if values[j] != values[j - 1]:
            out = jnp.where(i >= j, values[j], out)
    return out


def split_scaled(x):
    f = x.astype(jnp.float32) * SCALE
    hi = f.astype(jnp.bfloat16)
    lo = (f - hi.astype(jnp.float32)).astype(jnp.bfloat16)
    return jnp.concatenate([hi, lo], axis=1)


def scores(qq, k):
    return lax.dot_general(
        qq, jnp.concatenate([k, k], axis=1), (((1,), (1,)), ((), ())), preferred_element_type=jnp.float32
    )


def fold(s, v, m, a):
    top = jnp.maximum(m, jnp.max(s, axis=1, keepdims=True))
    p = jnp.exp2(s - top).astype(jnp.bfloat16)
    vv = jnp.concatenate([v, jnp.ones_like(v)], axis=1)
    a = a * jnp.exp2(m - top) + jnp.dot(p, vv, preferred_element_type=jnp.float32)
    return top, a


def kernel(
    q_ref, k_ref, v_ref, cos_ref, sin_ref, swap_ref, sk_ref, sv_ref, tq_ref, tk_ref, tv_ref, len_ref,
    out_ref, tout_ref,
    qh, kvh, qb, qq_s, kv, m_s, acc_s, o_send, l_send, o_recv, l_recv, out_stage, t_send, t_recv, t_stage,
    q_sem, kv_sem, near_sem, core_sem, far_sem, y_sem, o_sem, out_sem, t_sem, tg_sem,
):
    p = lax.axis_index("patch")
    h = lax.axis_index("head")
    x, y, c = p // 4, (p // 2) % 2, p % 2
    me = h * 2 + c
    rank = x * 2 + y

    def at(x_, y_, c_):
        return (x_ * 4 + y_ * 2 + c_, h)

    left, right = (x + 3) % 4, (x + 1) % 4
    lanes = pl.ds(pl.multiple_of(c * HD, HD), HD)

    barrier = pltpu.get_barrier_semaphore()

    def greet_plane(d, _):
        to = (me + d) % 16
        pl.semaphore_signal(barrier, inc=1, device_id=(x * 4 + y * 2 + to % 2, to // 2), device_id_type=MESH)
        return 0

    def greet_patch(d, _):
        to = (p + d) % 16
        pl.semaphore_signal(barrier, inc=1, device_id=(to, h), device_id_type=MESH)
        return 0

    lax.fori_loop(1, 16, greet_plane, 0)
    lax.fori_loop(1, 16, greet_patch, 0)
    pl.semaphore_wait(barrier, 30)

    def remote(src, dst, sems, index, to):
        return pltpu.make_async_remote_copy(
            src_ref=src, dst_ref=dst, send_sem=sems.at[(0,) + index], recv_sem=sems.at[(1,) + index],
            device_id=to, device_id_type=MESH,
        )

    def near(half, side, core, part):
        src = (sk_ref, sv_ref)[part].at[pl.ds(half * PIECE, PIECE), pl.ds(core * HD, HD)]
        piece = 4 + 4 * side + 2 * c + half
        return remote(src, kv.at[piece, part], near_sem, (side, c, half, part, core), at((right, left)[side], y, core))

    def near_arrives(half, side, core, part):
        piece = 4 + 4 * side + 2 * core + half
        ref = kv.at[piece, part]
        return remote(ref, ref, near_sem, (side, core, half, part, c), at(right, y, c))

    def near_each(half, fn):
        for side in range(2):
            for part in range(2):
                for core in range(2):
                    fn(half, side, core, part)

    near_each(0, lambda *a: near(*a).start())
    near_each(1, lambda *a: near(*a).start())

    other = pl.ds(pl.multiple_of((1 - c) * HD, HD), HD)

    def across(half, part):
        src = (sk_ref, sv_ref)[part].at[pl.ds(half * PIECE, PIECE), other]
        return remote(src, kv.at[2 * c + half, part], core_sem, (half, part), at(x, y, 1 - c))

    def across_arrives(half, part):
        ref = kv.at[2 * (1 - c) + half, part]
        return remote(ref, ref, core_sem, (half, part), at(x, y, 1 - c))

    cosine, sine, swap = cos_ref[...], sin_ref[...], swap_ref[...]

    def rotated(ref, g):
        value = ref[:, g * HD : (g + 1) * HD]
        turned = jnp.dot(value, swap, preferred_element_type=jnp.float32)
        return (value.astype(jnp.float32) * cosine + turned * sine).astype(jnp.bfloat16)

    def q_copy(d):
        to = (me + d) % 16
        return remote(qh.at[to], qb.at[c, h], q_sem, (d,), (x * 4 + y * 2 + to % 2, to // 2))

    def q_arrives(d):
        fr = (me + 16 - d) % 16
        ref = qb.at[fr % 2, fr // 2]
        return remote(ref, ref, q_sem, (d,), (x * 4 + y * 2 + fr % 2, fr // 2))

    def fresh_at(core, head):
        return kv.at[16 + 2 * core + head // 4, :, pl.ds(pl.multiple_of((head % 4) * BLOCK, BLOCK), BLOCK), :]

    def kv_copy(d):
        to = (me + d) % 16
        return remote(kvh.at[to], fresh_at(c, h), kv_sem, (d,), (x * 4 + y * 2 + to % 2, to // 2))

    def kv_arrives(d):
        fr = (me + 16 - d) % 16
        ref = fresh_at(fr % 2, fr // 2)
        return remote(ref, ref, kv_sem, (d,), (x * 4 + y * 2 + fr % 2, fr // 2))

    def loop(low, high, fn):
        def step(d, _):
            fn(d)
            return 0

        lax.fori_loop(low, high, step, 0)

    for g in range(16):
        qh[g] = rotated(q_ref, g)
    loop(1, 16, lambda d: q_copy(d).start())
    for g in range(16):
        kvh[g, 0] = rotated(k_ref, g)
        kvh[g, 1] = v_ref[:, g * HD : (g + 1) * HD]
    loop(1, 16, lambda d: kv_copy(d).start())
    for half in range(2):
        for part in range(2):
            across(half, part).start()

    for half in range(2):
        kv[2 * c + half, 0] = sk_ref[half * PIECE : (half + 1) * PIECE, lanes]
        kv[2 * c + half, 1] = sv_ref[half * PIECE : (half + 1) * PIECE, lanes]
    qb[c, h] = qh[me]
    row = pl.multiple_of((h % 4) * BLOCK, BLOCK)
    kv[16 + 2 * c + h // 4, :, pl.ds(row, BLOCK), :] = kvh[me]

    def clear(t):
        m_s[t] = jnp.full((TILE, HD), LOW, jnp.float32)
        acc_s[t] = jnp.zeros((TILE, 2 * HD), jnp.float32)

    loop(0, 4, clear)

    def ready(t):
        qq_s[t] = split_scaled(qb[t].reshape(TILE, HD))

    def y_copy(t):
        return remote(qb.at[t], qb.at[2 + t], y_sem, (t,), at(x, 1 - y, c))

    def y_arrives(t):
        return remote(qb.at[2 + t], qb.at[2 + t], y_sem, (t,), at(x, 1 - y, c))

    loop(1, 16, lambda d: q_arrives(d).wait_recv())
    for t in range(2):
        y_copy(t).start()
    loop(0, 2, ready)

    def far(half, core, part):
        src = kv.at[4 + 4 * part + 2 * core + half, part]
        dst = kv.at[12 + 2 * core + half, part]
        return remote(src, dst, far_sem, (core, half, part), at((right, left)[part], y, c))

    def far_arrives(half, core, part):
        ref = kv.at[12 + 2 * core + half, part]
        return remote(ref, ref, far_sem, (core, half, part), at(right, y, c))

    def near_ready(half):
        near_each(half, lambda *a: near_arrives(*a).wait_recv())
        for core in range(2):
            for part in range(2):
                far(half, core, part).start()

    valid = lax.broadcasted_iota(jnp.int32, (1, TXT), 1) < len_ref[0]

    def text_keys(t):
        s = jnp.where(valid, scores(qq_s[t], tk_ref[:, lanes]), LOW)
        m, a = fold(s, tv_ref[:, lanes], m_s[t][:, :1], acc_s[t])
        m_s[t] = jnp.broadcast_to(m, (TILE, HD))
        acc_s[t] = a

    def text_copy(d):
        to = (rank + d) % 8
        src = t_send.at[:, pl.ds(pl.multiple_of(to * 32, 32), 32), :]
        return remote(src, t_recv.at[rank], t_sem, (d,), at(to // 2, to % 2, c))

    def text_arrives(d):
        fr = (rank + 8 - d) % 8
        return remote(t_recv.at[fr], t_recv.at[fr], t_sem, (d,), at(fr // 2, fr % 2, c))

    def text_queries():
        qq = split_scaled(tq_ref[:, lanes])
        m = jnp.full((TXT, 1), LOW, jnp.float32)
        a = jnp.zeros((TXT, 2 * HD), jnp.float32)
        for piece in range(16, 20):
            m, a = fold(scores(qq, kv[piece, 0]), kv[piece, 1], m, a)
        here = valid & (rank == 0)
        s = jnp.where(here, scores(qq, tk_ref[:, lanes]), LOW)
        m, a = fold(s, tv_ref[:, lanes], m, a)
        total = a[:, HD:]
        t_send[0] = a[:, :HD] / total
        t_send[1] = m + jnp.log2(total)
        loop(1, 8, lambda d: text_copy(d).start())
        t_recv[rank] = t_send[:, pl.ds(pl.multiple_of(rank * 32, 32), 32), :]

    def gather_copy(d):
        to = (p + d) % 16
        dst = tout_ref.at[pl.ds(pl.multiple_of(rank * 32, 32), 32), lanes]
        return remote(t_stage, dst, tg_sem, (d,), (to, h))

    def gather_arrives(d):
        fr = (p + 16 - d) % 16
        rows = pl.ds(pl.multiple_of((fr // 2) * 32, 32), 32)
        ref = tout_ref.at[rows, pl.ds(pl.multiple_of((fr % 2) * HD, HD), HD)]
        return remote(ref, ref, tg_sem, (d,), (fr, h))

    def text_merge():
        loop(1, 8, lambda d: text_arrives(d).wait_recv())
        top = t_recv[0, 1]
        for r in range(1, 8):
            top = jnp.maximum(top, t_recv[r, 1])
        total = jnp.zeros((32, HD), jnp.float32)
        mixed = jnp.zeros((32, HD), jnp.float32)
        for r in range(8):
            w = jnp.exp2(t_recv[r, 1] - top)
            total += w
            mixed += w * t_recv[r, 0]
        done = (mixed / total).astype(jnp.bfloat16)
        t_stage[...] = done
        loop(1, 16, lambda d: gather_copy(d).start())
        tout_ref[pl.ds(pl.multiple_of(rank * 32, 32), 32), lanes] = done

    eye = lax.broadcasted_iota(jnp.int32, (HD, HD), 0) == lax.broadcasted_iota(jnp.int32, (HD, HD), 1)

    def o_copy(t):
        return remote(o_send.at[t], o_recv.at[t], o_sem, (t, 0), at(x, 1 - y, c))

    def l_copy(t):
        return remote(l_send.at[t], l_recv.at[t], o_sem, (t, 1), at(x, 1 - y, c))

    def give(t):
        total = acc_s[t][:, HD:]
        o_send[t - 2] = (acc_s[t][:, :HD] / total).astype(jnp.bfloat16)
        level = m_s[t] + jnp.log2(total)
        rows = []
        for b in range(TILE // HD):
            rows.append(jnp.sum(jnp.where(eye, level[b * HD : (b + 1) * HD], 0.0), axis=0, keepdims=True))
        l_send[t - 2] = jnp.concatenate(rows, axis=0)
        o_copy(t - 2).start()
        l_copy(t - 2).start()

    def out_copy(t, d):
        to = (h + d) % 8
        cols = pl.ds(pl.multiple_of(me * HD, HD), HD)
        return remote(out_stage.at[t, to], out_ref.at[:, cols], out_sem, (t, c, d), (x * 4 + y * 2 + t, to))

    def out_arrives(core, d):
        fr = (h + 8 - d) % 8
        ref = out_ref.at[:, pl.ds(pl.multiple_of((fr * 2 + core) * HD, HD), HD)]
        return remote(ref, ref, out_sem, (c, core, d), (x * 4 + y * 2 + core, fr))

    def take(t):
        o_copy(t).wait_recv()
        l_copy(t).wait_recv()
        total = acc_s[t][:, HD:]
        mine = acc_s[t][:, :HD] / total
        level = m_s[t] + jnp.log2(total)
        theirs = o_recv[t].astype(jnp.float32)
        got = l_recv[t]
        for b in range(TILE // HD):
            block = slice(b * HD, (b + 1) * HD)
            lev = jnp.sum(jnp.where(eye, got[b : b + 1], 0.0), axis=1, keepdims=True)
            top = jnp.maximum(level[block], lev)
            wa, wb = jnp.exp2(level[block] - top), jnp.exp2(lev - top)
            out_stage[t, b] = ((mine[block] * wa + theirs[block] * wb) / (wa + wb)).astype(jnp.bfloat16)
        first = (t + 2 - c) % 2

        loop(1, 8, lambda d: out_copy(t, d).start())

        @pl.when(first == 0)
        def _():
            out_ref[:, pl.ds(pl.multiple_of(me * HD, HD), HD)] = out_stage[t, h]

        @pl.when(first != 0)
        def _():
            out_copy(t, 0).start()

    def item(i):
        @pl.when(i == 0)
        def _():
            near_ready(0)

        @pl.when(i == 2)
        def _():
            loop(1, 16, lambda d: kv_arrives(d).wait_recv())
            for half in range(2):
                for part in range(2):
                    across_arrives(half, part).wait_recv()

        @pl.when(i == 4)
        def _():
            near_ready(1)

        @pl.when(i == 6)
        def _():
            loop(0, 2, text_keys)
            text_queries()
            for t in range(2):
                y_arrives(t).wait_recv()
            loop(2, 4, ready)

        @pl.when(i == 9)
        def _():
            text_merge()

        @pl.when(i == 12)
        def _():
            for half in range(2):
                for core in range(2):
                    for part in range(2):
                        far_arrives(half, core, part).wait_recv()

        t = pick(i, [q for q, _ in ITEMS])
        ids = [pick(i, [pieces[n] for _, pieces in ITEMS]) for n in range(4)]
        qq = qq_s[t]
        m = m_s[t][:, :1]
        a = acc_s[t]
        s = scores(qq, kv[ids[0], 0])
        for n in range(4):
            following = scores(qq, kv[ids[n + 1], 0]) if n < 3 else None
            m, a = fold(s, kv[ids[n], 1], m, a)
            s = following
        m_s[t] = jnp.broadcast_to(m, (TILE, HD))
        acc_s[t] = a

        @pl.when((i >= 12) & (i < 14))
        def _():
            give(t)

        @pl.when(i >= 14)
        def _():
            take(t)

    loop(0, 16, item)

    loop(1, 16, lambda d: gather_arrives(d).wait_recv())
    loop(1, 8, lambda d: out_arrives(c, d).wait_recv())
    loop(0, 8, lambda d: out_arrives(1 - c, d).wait_recv())
    near_each(0, lambda *a: near(*a).wait_send())
    near_each(1, lambda *a: near(*a).wait_send())
    loop(1, 16, lambda d: q_copy(d).wait_send())
    loop(1, 16, lambda d: kv_copy(d).wait_send())
    for half in range(2):
        for part in range(2):
            across(half, part).wait_send()
            for core in range(2):
                far(half, core, part).wait_send()
    for t in range(2):
        y_copy(t).wait_send()
        o_copy(t).wait_send()
        l_copy(t).wait_send()
    loop(1, 8, lambda d: text_copy(d).wait_send())
    loop(1, 16, lambda d: gather_copy(d).wait_send())
    loop(1, 8, lambda d: out_copy(c, d).wait_send())
    loop(0, 8, lambda d: out_copy(1 - c, d).wait_send())


def body(image_query, image_key, image_value, positions, stale_key, stale_value, text_query, text_key, text_value, text_len):
    freqs, which, swap = rotation_tables()
    pos = positions.astype(jnp.float32)
    angles = jnp.take(pos, jnp.asarray(which), axis=0).T * jnp.asarray(freqs)[None, :]
    dma = pltpu.SemaphoreType.DMA
    bf, f32 = jnp.bfloat16, jnp.float32
    vmem = pl.BlockSpec(memory_space=pltpu.VMEM)
    return pl.pallas_call(
        kernel,
        out_shape=(
            jax.ShapeDtypeStruct(image_query.shape, bf),
            jax.ShapeDtypeStruct(text_query.shape, bf),
        ),
        in_specs=[vmem] * 11 + [pl.BlockSpec(memory_space=pltpu.SMEM)],
        out_specs=(vmem, vmem),
        scratch_shapes=[
            pltpu.VMEM((16, BLOCK, HD), bf),
            pltpu.VMEM((16, 2, BLOCK, HD), bf),
            pltpu.VMEM((4, 8, BLOCK, HD), bf),
            pltpu.VMEM((4, TILE, 2 * HD), bf),
            pltpu.VMEM((20, 2, PIECE, HD), bf),
            pltpu.VMEM((4, TILE, HD), f32),
            pltpu.VMEM((4, TILE, 2 * HD), f32),
            pltpu.VMEM((2, TILE, HD), bf),
            pltpu.VMEM((2, 8, HD), f32),
            pltpu.VMEM((2, TILE, HD), bf),
            pltpu.VMEM((2, 8, HD), f32),
            pltpu.VMEM((2, 8, BLOCK, HD), bf),
            pltpu.VMEM((2, TXT, HD), f32),
            pltpu.VMEM((8, 2, 32, HD), f32),
            pltpu.VMEM((32, HD), bf),
            dma((2, 16)),
            dma((2, 16)),
            dma((2, 2, 2, 2, 2, 2)),
            dma((2, 2, 2)),
            dma((2, 2, 2, 2)),
            dma((2, 2)),
            dma((2, 2, 2)),
            dma((2, 2, 2, 8)),
            dma((2, 8)),
            dma((2, 16)),
        ],
        compiler_params=pltpu.CompilerParams(
            collective_id=0, has_side_effects=True, vmem_limit_bytes=56 * 2**20
        ),
        name="joint_attention",
    )(
        image_query, image_key, image_value, jnp.cos(angles), jnp.sin(angles), jnp.asarray(swap, bf),
        stale_key, stale_value, text_query, text_key, text_value, text_len,
    )


def solution(mesh):
    return jax.shard_map(
        body,
        mesh=mesh,
        in_specs=(
            P(("patch", "head"), None),
            P(("patch", "head"), None),
            P(("patch", "head"), None),
            P(None, ("patch", "head")),
            P("patch", "head"),
            P("patch", "head"),
            P(None, "head"),
            P(None, "head"),
            P(None, "head"),
            P(),
        ),
        out_specs=(P(("patch", "head"), None), P(None, "head")),
        check_vma=False,
    )
```

time: 433 us -> 148 us (0.34)
  Pallas kernels: 0 us -> 141 us
  waiting for transfers between devices: 133 us -> 0 us
  matrix products: 90.1 us -> 0 us
  other arithmetic: 68.4 us -> 1.59 us
  local copies, waits for them, and re-layouts: 56.7 us -> 3.87 us
  blocking collectives: 45.4 us -> 0 us
  starting transfers between devices: 21.4 us -> 0 us
  between operations: 14.8 us -> 1.32 us
    pallas_call x0 -> x1, Pallas kernels: none -> 141 us  [body(): pl.pallas_call(kernel, out_shape=(jax.ShapeDtypeStruct(image_query.shape,...]
    all_gather x3 -> x0, waiting for transfers between devices: 125 us -> none  [the longest x1 73.1 us: body(): lax.all_gather(stale_value, 'patch', axis=0, tiled=True)]
    dot_general x40 -> x0, matrix products: 90.1 us -> none  [the longest x20 49.5 us: fold_block(): jnp.einsum('hqk,khd->hqd', weights.astype(jnp.bfloat16), values, preferre...]
    all_gather x2 -> x0, blocking collectives: 45.4 us -> none  [joined(): pieces = jax.tree.map(lambda part: lax.all_gather(part, axis), value)]
    reduce_sum x20 -> x0, other arithmetic: 41.9 us -> none  [fold_block(): total = total * keep + jnp.sum(weights, axis=2)]
    all_to_all x4 -> x0, starting transfers between devices: 21.3 us -> none  [the longest x1 6.88 us: body(): lax.all_to_all(rotated_key, 'head', split_axis=1, concat_axis=0, tiled=True)]
    dynamic_slice x16 -> x0, local copies, waits for them, and re-layouts: 20.4 us -> none  [step(): values = lax.dynamic_slice_in_dim(gathered_value, offset, block, 0)]
    add x48 -> x0, other arithmetic: 19.6 us -> none  [the longest x15 18.1 us: combine_states(): first[2] * left[:, :, None] + second[2] * right[:, :, None]]
  transfers between devices with their start and end apart: 7 -> 0, of which waited for: 4 -> 0; matrix products, arithmetic and copies ran while one was open for 13% -> 0% of each run, Pallas kernels for 0% -> 0%
where the time goes in v1:
time: 148 us
  Pallas kernels  141 us (95%)
  local copies, waits for them, and re-layouts  3.87 us (3%)
  other arithmetic  1.59 us (1%)
    pallas_call x1, Pallas kernels, body(): pl.pallas_call(kernel, out_shape=(jax.ShapeDtypeStruct(image_query.shape,...  141 us
    unnamed x8, local copies, waits for them, and re-layouts  3.14 us

profile of v1, /device:TPU:1, one launch (start us, length us, event | category | flops | bytes accessed | tf_op | source)
XLA Modules:
  0.0 147.9 jit_solution(14598129866024396631)
XLA Ops:
  1.3 0.0 copy-start.2
  1.3 0.7 convert_element_type.3
  2.0 0.0 copy-done.2
  2.0 0.6 gather_fusion
  2.6 0.0 copy-start.1
  2.6 0.1 copy.15
  2.7 0.6 copy-done.1
  3.3 0.9 sine_bitcast_fusion
  4.2 141.1 %joint_attention.1 = (bf16[128,2048]{1,0:T(8,128)(2,1)}, bf16[256,256]{1,0:T(8,128)(2,1)}) custom-call(bf16[128,2048]{1,0:T(8,128)(2,1)} %q_ref.1, bf16[128,2048]{1,0:T(8,128)(2,1)} %k_ref.1, bf16[128,2048]{1,0:T(8,128)(2,1)} %v_ref.1, f32[128,128]{1,0:T(8,128)} %get-tuple-element.3.cos_ref, f32[128,128]{1,0:T(8,128)} %get-tuple-element.2.sin_ref, ...), custom_call_target="tpu_custom_call" | custom-call | tf_op jit(solution)/shard_map/joint_attention/pallas_call | solution.py:440
  145.3 0.0 copy-start
  145.3 1.9 %copy.19 = bf16[128,2048]{1,0:T(8,128)(2,1)} copy(bf16[128,2048]{1,0:T(8,128)(2,1)} %get-tuple-element.6) | data formatting | bytes 1048576
  147.2 0.0 copy-done
  147.3 0.7 copy.20
  (1 shorter events, 0.0 us)
Async XLA Ops:
  1.3 0.7 copy-start.2
  2.6 0.7 copy-start.1
  145.3 1.9 %copy-start = (bf16[256,256]{1,0:T(8,128)(2,1)S(1)}, bf16[256,256]{1,0:T(8,128)(2,1)}, u32[]{:S(2)}) copy-start(bf16[256,256]{1,0:T(8,128)(2,1)} %get-tuple-element.7) | copy-start | bytes 393220

commit v2 on v1

--- a/solution.py
+++ b/solution.py
@@ -34,20 +34,23 @@
 def rotation_tables():
     first = HD // 8
     second = (HD - first) // 2
-    freqs = np.zeros((HD,), np.float32)
-    which = np.zeros((HD,), np.int32)
+    freqs = np.zeros((3, HD), np.float32)
     swap = np.zeros((HD, HD), np.float32)
     begin = 0
     for axis_id, width in enumerate([first, second, HD - first - second]):
         half = width // 2
         for index in range(half):
             low, high = begin + index, begin + index + half
-            freqs[low] = freqs[high] = np.float32(THETA ** (-2.0 * index / width))
-            which[low] = which[high] = axis_id
+            freqs[axis_id, low] = freqs[axis_id, high] = np.float32(THETA ** (-2.0 * index / width))
             swap[high, low] = -1.0
             swap[low, high] = 1.0
         begin += width
-    return freqs, which, swap
+    terms = []
+    for _ in range(3):
+        term = freqs.astype(jnp.bfloat16)
+        terms.append(term)
+        freqs = freqs - term.astype(np.float32)
+    return np.concatenate(terms + [np.zeros((7, HD), jnp.bfloat16)], axis=0), swap
 
 
 def pick(i, values):
@@ -80,7 +83,7 @@
 
 
 def kernel(
-    q_ref, k_ref, v_ref, cos_ref, sin_ref, swap_ref, sk_ref, sv_ref, tq_ref, tk_ref, tv_ref, len_ref,
+    q_ref, k_ref, v_ref, pos_ref, freq_ref, swap_ref, sk_ref, sv_ref, tq_ref, tk_ref, tv_ref, len_ref,
     out_ref, tout_ref,
     qh, kvh, qb, qq_s, kv, m_s, acc_s, o_send, l_send, o_recv, l_recv, out_stage, t_send, t_recv, t_stage,
     q_sem, kv_sem, near_sem, core_sem, far_sem, y_sem, o_sem, out_sem, t_sem, tg_sem,
@@ -99,19 +102,10 @@
 
     barrier = pltpu.get_barrier_semaphore()
 
-    def greet_plane(d, _):
+    for d in range(1, 16):
         to = (me + d) % 16
         pl.semaphore_signal(barrier, inc=1, device_id=(x * 4 + y * 2 + to % 2, to // 2), device_id_type=MESH)
-        return 0
-
-    def greet_patch(d, _):
-        to = (p + d) % 16
-        pl.semaphore_signal(barrier, inc=1, device_id=(to, h), device_id_type=MESH)
-        return 0
-
-    lax.fori_loop(1, 16, greet_plane, 0)
-    lax.fori_loop(1, 16, greet_patch, 0)
-    pl.semaphore_wait(barrier, 30)
+        pl.semaphore_signal(barrier, inc=1, device_id=((p + d) % 16, h), device_id_type=MESH)
 
     def remote(src, dst, sems, index, to):
         return pltpu.make_async_remote_copy(
@@ -135,9 +129,6 @@
                 for core in range(2):
                     fn(half, side, core, part)
 
-    near_each(0, lambda *a: near(*a).start())
-    near_each(1, lambda *a: near(*a).start())
-
     other = pl.ds(pl.multiple_of((1 - c) * HD, HD), HD)
 
     def across(half, part):
@@ -148,7 +139,11 @@
         ref = kv.at[2 * (1 - c) + half, part]
         return remote(ref, ref, core_sem, (half, part), at(x, y, 1 - c))
 
-    cosine, sine, swap = cos_ref[...], sin_ref[...], swap_ref[...]
+    swap = swap_ref[...]
+    pos = pos_ref[...].astype(jnp.float32)
+    pos = jnp.concatenate([pos, pos, pos, jnp.zeros((7, BLOCK), jnp.float32)], axis=0).astype(jnp.bfloat16)
+    angle = lax.dot_general(pos, freq_ref[...], (((0,), (0,)), ((), ())), preferred_element_type=jnp.float32)
+    cosine, sine = jnp.cos(angle), jnp.sin(angle)
 
     def rotated(ref, g):
         value = ref[:, g * HD : (g + 1) * HD]
@@ -185,11 +180,15 @@
 
     for g in range(16):
         qh[g] = rotated(q_ref, g)
-    loop(1, 16, lambda d: q_copy(d).start())
     for g in range(16):
         kvh[g, 0] = rotated(k_ref, g)
         kvh[g, 1] = v_ref[:, g * HD : (g + 1) * HD]
+
+    pl.semaphore_wait(barrier, 30)
+    loop(1, 16, lambda d: q_copy(d).start())
+    near_each(0, lambda *a: near(*a).start())
     loop(1, 16, lambda d: kv_copy(d).start())
+    near_each(1, lambda *a: near(*a).start())
     for half in range(2):
         for part in range(2):
             across(half, part).start()
@@ -240,7 +239,7 @@
 
     def text_keys(t):
         s = jnp.where(valid, scores(qq_s[t], tk_ref[:, lanes]), LOW)
-        m, a = fold(s, tv_ref[:, lanes], m_s[t][:, :1], acc_s[t])
+        m, a = fold(s, tv_ref[:, lanes], jnp.max(m_s[t], axis=1, keepdims=True), acc_s[t])
         m_s[t] = jnp.broadcast_to(m, (TILE, HD))
         acc_s[t] = a
 
@@ -388,7 +387,7 @@
         t = pick(i, [q for q, _ in ITEMS])
         ids = [pick(i, [pieces[n] for _, pieces in ITEMS]) for n in range(4)]
         qq = qq_s[t]
-        m = m_s[t][:, :1]
+        m = jnp.max(m_s[t], axis=1, keepdims=True)
         a = acc_s[t]
         s = scores(qq, kv[ids[0], 0])
         for n in range(4):
@@ -431,9 +430,7 @@
 
 
 def body(image_query, image_key, image_value, positions, stale_key, stale_value, text_query, text_key, text_value, text_len):
-    freqs, which, swap = rotation_tables()
-    pos = positions.astype(jnp.float32)
-    angles = jnp.take(pos, jnp.asarray(which), axis=0).T * jnp.asarray(freqs)[None, :]
+    freqs, swap = rotation_tables()
     dma = pltpu.SemaphoreType.DMA
     bf, f32 = jnp.bfloat16, jnp.float32
     vmem = pl.BlockSpec(memory_space=pltpu.VMEM)
@@ -477,7 +474,7 @@
         ),
         name="joint_attention",
     )(
-        image_query, image_key, image_value, jnp.cos(angles), jnp.sin(angles), jnp.asarray(swap, bf),
+        image_query, image_key, image_value, positions, jnp.asarray(freqs), jnp.asarray(swap, bf),
         stale_key, stale_value, text_query, text_key, text_value, text_len,
     )
 

time: 148 us -> 95 us (0.64)
  Pallas kernels: 141 us -> 91 us
  other arithmetic: 1.59 us -> 0 us
    pallas_call x1, Pallas kernels: 141 us -> 91 us  [body(): pl.pallas_call(kernel, out_shape=(jax.ShapeDtypeStruct(image_query.shape,...]
    unnamed x8 -> x4, local copies, waits for them, and re-layouts: 3.14 us -> 2.58 us
where the time goes in v2:
time: 95 us; the launch traced here: 94.8 us
  Pallas kernels  91 us (96%)
  local copies, waits for them, and re-layouts  2.58 us (3%)
  between operations  1.3 us (1%)
    pallas_call x1, Pallas kernels, body(): pl.pallas_call(kernel, out_shape=(jax.ShapeDtypeStruct(image_query.shape,...  91 us
    unnamed x4, local copies, waits for them, and re-layouts  2.58 us

profile of v2, /device:TPU:1, one launch (start us, length us, event | category | flops | bytes accessed | tf_op | source)
XLA Modules:
  0.0 94.8 jit_solution(2356471548842743594)
XLA Ops:
  1.3 91.0 %joint_attention.1 = (bf16[128,2048]{1,0:T(8,128)(2,1)}, bf16[256,256]{1,0:T(8,128)(2,1)}) custom-call(bf16[128,2048]{1,0:T(8,128)(2,1)} %q_ref.1, bf16[128,2048]{1,0:T(8,128)(2,1)} %k_ref.1, bf16[128,2048]{1,0:T(8,128)(2,1)} %v_ref.1, s32[3,128]{1,0:T(4,128)} %pos_ref.1, bf16[16,128]{1,0:T(8,128)(2,1)} %constant.4.clone.freq_ref, ...), custom_call_target="tpu_custom_call" | custom-call | tf_op jit(solution)/shard_map/joint_attention/pallas_call | solution.py:437
  92.2 0.0 copy-start
  92.3 1.9 %copy.17 = bf16[128,2048]{1,0:T(8,128)(2,1)} copy(bf16[128,2048]{1,0:T(8,128)(2,1)} %get-tuple-element.4) | data formatting | bytes 1048576
  94.2 0.0 copy-done
  94.2 0.7 copy.18
Async XLA Ops:
  92.2 1.9 %copy-start = (bf16[256,256]{1,0:T(8,128)(2,1)S(1)}, bf16[256,256]{1,0:T(8,128)(2,1)}, u32[]{:S(2)}) copy-start(bf16[256,256]{1,0:T(8,128)(2,1)} %get-tuple-element.5) | copy-start | bytes 393220

commit v3 on v2

v3 whole, which is shorter than its diff:
```python
import functools

import jax
import jax.numpy as jnp
import numpy as np
from jax import lax
from jax.experimental import pallas as pl
from jax.experimental.pallas import tpu as pltpu
from jax.sharding import PartitionSpec as P

HD = 128
THETA = 256.0
MESH = pl.DeviceIdType.MESH
SCALE = 1.4426950408889634 * HD ** (-0.5)
LOW = -1e30
TILE = 1024
PIECE = 512
BLOCK = 128
TXT = 256

NEAR_A, NEAR_B, FAR, OWN = (4, 6, 8, 10), (5, 7, 9, 11), (12, 13, 14, 15), (0, 1, 2, 3)
ITEMS = [
    (0, NEAR_A), (1, NEAR_A),
    (2, OWN), (3, OWN),
    (2, NEAR_A), (3, NEAR_A),
    (2, NEAR_B), (3, NEAR_B),
    (2, FAR), (3, FAR),
    (0, NEAR_B), (0, FAR),
    (1, NEAR_B), (1, FAR),
]
ORDER16 = [1, 9, 2, 10, 3, 11, 4, 12, 5, 13, 6, 14, 7, 15, 8]
ORDER8 = [4, 1, 5, 2, 6, 3, 7, 0]


def rotation_tables():
    first = HD // 8
    second = (HD - first) // 2
    freqs = np.zeros((3, HD), np.float32)
    swap = np.zeros((HD, HD), np.float32)
    begin = 0
    for axis_id, width in enumerate([first, second, HD - first - second]):
        half = width // 2
        for index in range(half):
            low, high = begin + index, begin + index + half
            freqs[axis_id, low] = freqs[axis_id, high] = np.float32(THETA ** (-2.0 * index / width))
            swap[high, low] = -1.0
            swap[low, high] = 1.0
        begin += width
    terms = []
    for _ in range(3):
        term = freqs.astype(jnp.bfloat16)
        terms.append(term)
        freqs = freqs - term.astype(np.float32)
    return np.concatenate(terms + [np.zeros((7, HD), jnp.bfloat16)], axis=0), swap


def pick(i, values):
    out = values[0]
    for j in range(1, len(values)):
        if values[j] != values[j - 1]:
            out = jnp.where(i >= j, values[j], out)
    return out


def split_scaled(x):
    f = x.astype(jnp.float32) * SCALE
    hi = f.astype(jnp.bfloat16)
    lo = (f - hi.astype(jnp.float32)).astype(jnp.bfloat16)
    return jnp.concatenate([hi, lo], axis=1)


def scores(qq, k):
    return lax.dot_general(
        qq, jnp.concatenate([k, k], axis=1), (((1,), (1,)), ((), ())), preferred_element_type=jnp.float32
    )


def fold(s, v, m, a):
    top = jnp.maximum(m, jnp.max(s, axis=1, keepdims=True))
    p = jnp.exp2(s - top).astype(jnp.bfloat16)
    vv = jnp.concatenate([v, jnp.ones_like(v)], axis=1)
    a = a * jnp.exp2(m - top) + jnp.dot(p, vv, preferred_element_type=jnp.float32)
    return top, a


def kernel(
    q_in, k_in, v_in, pos_ref, freq_ref, swap_ref, sk_ref, sv_ref, tq_ref, tk_ref, tv_ref, len_ref,
    out_ref, tout_ref,
    q_ref, k_ref, v_ref, qh, kvh, qb, qq_s, kv, m_s, acc_s, o_send, l_send, o_recv, l_recv, out_stage, t_send, t_recv, t_stage,
    in_sem, q_sem, kv_sem, near_sem, core_sem, far_sem, y_sem, o_sem, out_sem, t_sem, tg_sem,
):
    p = lax.axis_index("patch")
    h = lax.axis_index("head")
    x, y, c = p // 4, (p // 2) % 2, p % 2
    me = h * 2 + c
    rank = x * 2 + y

    def at(x_, y_, c_):
        return (x_ * 4 + y_ * 2 + c_, h)

    left, right = (x + 3) % 4, (x + 1) % 4
    lanes = pl.ds(pl.multiple_of(c * HD, HD), HD)

    barrier = pltpu.get_barrier_semaphore()

    for d in range(1, 16):
        to = (me + d) % 16
        pl.semaphore_signal(barrier, inc=1, device_id=(x * 4 + y * 2 + to % 2, to // 2), device_id_type=MESH)
        pl.semaphore_signal(barrier, inc=1, device_id=((p + d) % 16, h), device_id_type=MESH)

    loads = [pltpu.make_async_copy(a, b, in_sem.at[n]) for n, (a, b) in enumerate(((q_in, q_ref), (k_in, k_ref), (v_in, v_ref)))]
    for half in range(2):
        for part in range(2):
            src = (sk_ref, sv_ref)[part].at[pl.ds(half * PIECE, PIECE), lanes]
            loads.append(pltpu.make_async_copy(src, kv.at[2 * c + half, part], in_sem.at[3 + 2 * half + part]))
    for load in loads:
        load.start()

    def remote(src, dst, sems, index, to):
        return pltpu.make_async_remote_copy(
            src_ref=src, dst_ref=dst, send_sem=sems.at[(0,) + index], recv_sem=sems.at[(1,) + index],
            device_id=to, device_id_type=MESH,
        )

    def whole(ref, sems, index=()):
        return remote(ref, ref, sems, index, at(x, y, 1 - c))

    def near(half, side, core, part):
        src = (sk_ref, sv_ref)[part].at[pl.ds(half * PIECE, PIECE), pl.ds(core * HD, HD)]
        piece = 4 + 4 * side + 2 * c + half
        return remote(src, kv.at[piece, part], near_sem, (half,), at((right, left)[side], y, core))

    def near_each(half, fn):
        for side in range(2):
            for part in range(2):
                for core in range(2):
                    fn(half, side, core, part)

    other = pl.ds(pl.multiple_of((1 - c) * HD, HD), HD)

    def across(half, part):
        src = (sk_ref, sv_ref)[part].at[pl.ds(half * PIECE, PIECE), other]
        return remote(src, kv.at[2 * c + half, part], core_sem, (), at(x, y, 1 - c))

    swap = swap_ref[...]
    pos = pos_ref[...].astype(jnp.float32)
    pos = jnp.concatenate([pos, pos, pos, jnp.zeros((7, BLOCK), jnp.float32)], axis=0).astype(jnp.bfloat16)
    angle = lax.dot_general(pos, freq_ref[...], (((0,), (0,)), ((), ())), preferred_element_type=jnp.float32)
    cosine, sine = jnp.cos(angle), jnp.sin(angle)

    def rotated(ref, g):
        value = ref[:, g * HD : (g + 1) * HD]
        turned = jnp.dot(value, swap, preferred_element_type=jnp.float32)
        return (value.astype(jnp.float32) * cosine + turned * sine).astype(jnp.bfloat16)

    def q_copy(d):
        to = (me + d) % 16
        return remote(qh.at[to], qb.at[c, h], q_sem, (), (x * 4 + y * 2 + to % 2, to // 2))

    def fresh_at(core, head):
        return kv.at[16 + 2 * core + head // 4, :, pl.ds(pl.multiple_of((head % 4) * BLOCK, BLOCK), BLOCK), :]

    def kv_copy(d):
        to = (me + d) % 16
        return remote(kvh.at[to], fresh_at(c, h), kv_sem, (), (x * 4 + y * 2 + to % 2, to // 2))

    def loop(low, high, fn):
        def step(d, _):
            fn(d)
            return 0

        lax.fori_loop(low, high, step, 0)

    loads[0].wait()
    for g in range(16):
        qh[g] = rotated(q_ref, g)
    loads[1].wait()
    loads[2].wait()
    for g in range(16):
        kvh[g, 0] = rotated(k_ref, g)
        kvh[g, 1] = v_ref[:, g * HD : (g + 1) * HD]

    for load in loads[3:]:
        load.wait()
    pl.semaphore_wait(barrier, 30)
    for d in ORDER16:
        q_copy(d).start()
    near_each(0, lambda *a: near(*a).start())
    for half in range(2):
        for part in range(2):
            across(half, part).start()
    for d in ORDER16:
        kv_copy(d).start()
    near_each(1, lambda *a: near(*a).start())

    qb[c, h] = qh[me]
    row = pl.multiple_of((h % 4) * BLOCK, BLOCK)
    kv[16 + 2 * c + h // 4, :, pl.ds(row, BLOCK), :] = kvh[me]

    def clear(t):
        m_s[t] = jnp.full((TILE, HD), LOW, jnp.float32)
        acc_s[t] = jnp.zeros((TILE, 2 * HD), jnp.float32)

    loop(0, 4, clear)

    def ready(t):
        qq_s[t] = split_scaled(qb[t].reshape(TILE, HD))

    def y_copy(t):
        return remote(qb.at[t], qb.at[2 + t], y_sem, (), at(x, 1 - y, c))

    whole(qh.at[pl.ds(0, 15)], q_sem).wait_recv()
    for t in range(2):
        y_copy(t).start()
    loop(0, 2, ready)

    def far(half, core, part):
        src = kv.at[4 + 4 * part + 2 * core + half, part]
        dst = kv.at[12 + 2 * core + half, part]
        return remote(src, dst, far_sem, (), at((right, left)[part], y, c))

    def near_ready(half):
        whole(kv.at[pl.ds(4, 4)], near_sem, (half,)).wait_recv()
        for core in range(2):
            for part in range(2):
                far(half, core, part).start()

    valid = lax.broadcasted_iota(jnp.int32, (1, TXT), 1) < len_ref[0]

    def attend(t, ids, text=False):
        qq = qq_s[t]
        m = jnp.max(m_s[t], axis=1, keepdims=True)
        a = acc_s[t]
        keys = [lambda n=n: scores(qq, kv[ids[n], 0]) for n in range(len(ids))]
        values = [lambda n=n: kv[ids[n], 1] for n in range(len(ids))]
        if text:
            keys.append(lambda: jnp.where(valid, scores(qq, tk_ref[:, lanes]), LOW))
            values.append(lambda: tv_ref[:, lanes])
        s = keys[0]()
        for n in range(len(keys)):
            following = keys[n + 1]() if n + 1 < len(keys) else None
            m, a = fold(s, values[n](), m, a)
            s = following
        m_s[t] = jnp.broadcast_to(m, (TILE, HD))
        acc_s[t] = a

    def text_copy(d):
        to = (rank + d) % 8
        src = t_send.at[:, pl.ds(pl.multiple_of(to * 32, 32), 32), :]
        return remote(src, t_recv.at[rank], t_sem, (), at(to // 2, to % 2, c))

    def text_queries():
        qq = split_scaled(tq_ref[:, lanes])
        m = jnp.full((TXT, 1), LOW, jnp.float32)
        a = jnp.zeros((TXT, 2 * HD), jnp.float32)
        for piece in range(16, 20):
            m, a = fold(scores(qq, kv[piece, 0]), kv[piece, 1], m, a)
        here = valid & (rank == 0)
        s = jnp.where(here, scores(qq, tk_ref[:, lanes]), LOW)
        m, a = fold(s, tv_ref[:, lanes], m, a)
        total = a[:, HD:]
        t_send[0] = a[:, :HD] / total
        t_send[1] = m + jnp.log2(total)
        loop(1, 8, lambda d: text_copy(d).start())
        t_recv[rank] = t_send[:, pl.ds(pl.multiple_of(rank * 32, 32), 32), :]

    def gather_copy(d):
        to = (p + d) % 16
        dst = tout_ref.at[pl.ds(pl.multiple_of(rank * 32, 32), 32), lanes]
        return remote(t_stage, dst, tg_sem, (), (to, h))

    def text_merge():
        whole(t_recv.at[pl.ds(0, 7)], t_sem).wait_recv()
        top = t_recv[0, 1]
        for r in range(1, 8):
            top = jnp.maximum(top, t_recv[r, 1])
        total = jnp.zeros((32, HD), jnp.float32)
        mixed = jnp.zeros((32, HD), jnp.float32)
        for r in range(8):
            w = jnp.exp2(t_recv[r, 1] - top)
            total += w
            mixed += w * t_recv[r, 0]
        done = (mixed / total).astype(jnp.bfloat16)
        t_stage[...] = done
        loop(1, 16, lambda d: gather_copy(d).start())
        tout_ref[pl.ds(pl.multiple_of(rank * 32, 32), 32), lanes] = done

    eye = lax.broadcasted_iota(jnp.int32, (HD, HD), 0) == lax.broadcasted_iota(jnp.int32, (HD, HD), 1)

    def o_copy(t):
        return remote(o_send.at[t], o_recv.at[t], o_sem, (t, 0), at(x, 1 - y, c))

    def l_copy(t):
        return remote(l_send.at[t], l_recv.at[t], o_sem, (t, 1), at(x, 1 - y, c))

    def give(t):
        total = acc_s[t][:, HD:]
        o_send[t - 2] = (acc_s[t][:, :HD] / total).astype(jnp.bfloat16)
        level = m_s[t] + jnp.log2(total)
        rows = []
        for b in range(TILE // HD):
            rows.append(jnp.sum(jnp.where(eye, level[b * HD : (b + 1) * HD], 0.0), axis=0, keepdims=True))
        l_send[t - 2] = jnp.concatenate(rows, axis=0)
        o_copy(t - 2).start()
        l_copy(t - 2).start()

    def out_copy(t, d):
        to = (h + d) % 8
        cols = pl.ds(pl.multiple_of(me * HD, HD), HD)
        return remote(out_stage.at[t, to], out_ref.at[:, cols], out_sem, (), (x * 4 + y * 2 + t, to))

    def take(t):
        o_copy(t).wait_recv()
        l_copy(t).wait_recv()
        own = jnp.where(t == c, 0, 1)
        for d in ORDER8:
            b = (h + d) % 8
            rows = pl.ds(pl.multiple_of(b * HD, HD), HD)
            total = acc_s[t, rows, HD:]
            level = m_s[t, rows] + jnp.log2(total)
            lev = jnp.sum(jnp.where(eye, l_recv[t, pl.ds(b, 1)], 0.0), axis=1, keepdims=True)
            top = jnp.maximum(level, lev)
            wa, wb = jnp.exp2(level - top), jnp.exp2(lev - top)
            mixed = acc_s[t, rows, :HD] * (wa / total) + o_recv[t, rows].astype(jnp.float32) * wb
            out_stage[t, b] = (mixed / (wa + wb)).astype(jnp.bfloat16)
            if d != 0:
                out_copy(t, d).start()

        @pl.when(own != 0)
        def _():
            out_copy(t, 0).start()

        @pl.when(own == 0)
        def _():
            out_ref[:, pl.ds(pl.multiple_of(me * HD, HD), HD)] = out_stage[t, h]

    def item(i):
        @pl.when(i == 0)
        def _():
            near_ready(0)

        @pl.when(i == 2)
        def _():
            whole(kvh.at[pl.ds(0, 15)], kv_sem).wait_recv()
            loop(0, 2, lambda t: attend(t, (16 + 2 * t, 17 + 2 * t)))
            near_ready(1)
            text_queries()
            whole(qb.at[pl.ds(2, 2)], y_sem).wait_recv()
            loop(2, 4, ready)

        @pl.when(i == 5)
        def _():
            text_merge()

        @pl.when(i == 8)
        def _():
            whole(kv.at[pl.ds(12, 4)], far_sem).wait_recv()

        t = pick(i, [q for q, _ in ITEMS])
        ids = [pick(i, [pieces[n] for _, pieces in ITEMS]) for n in range(4)]
        attend(t, ids)

        @pl.when((i >= 8) & (i < 10))
        def _():
            give(t)

        @pl.when((i == 11) | (i == 13))
        def _():
            take(t)

    whole(kv.at[pl.ds(0, 2)], core_sem).wait_recv()
    loop(0, 2, lambda t: attend(t, (2 - 2 * t, 3 - 2 * t), text=True))
    loop(0, 14, item)

    for half in range(2):
        whole(kv.at[pl.ds(4, 4)], near_sem, (half,)).wait_send()
    whole(qh.at[pl.ds(0, 15)], q_sem).wait_send()
    whole(kvh.at[pl.ds(0, 15)], kv_sem).wait_send()
    whole(kv.at[pl.ds(0, 2)], core_sem).wait_send()
    whole(kv.at[pl.ds(12, 4)], far_sem).wait_send()
    whole(qb.at[pl.ds(2, 2)], y_sem).wait_send()
    for t in range(2):
        o_copy(t).wait_send()
        l_copy(t).wait_send()
    whole(t_recv.at[pl.ds(0, 7)], t_sem).wait_send()
    whole(qh.at[pl.ds(0, 15), pl.ds(0, 32)], tg_sem).wait_send()
    whole(qh.at[pl.ds(0, 15), pl.ds(0, 32)], tg_sem).wait_recv()
    whole(qh.at[pl.ds(0, 15)], out_sem).wait_send()
    whole(qh.at[pl.ds(0, 15)], out_sem).wait_recv()


def body(image_query, image_key, image_value, positions, stale_key, stale_value, text_query, text_key, text_value, text_len):
    freqs, swap = rotation_tables()
    dma = pltpu.SemaphoreType.DMA
    bf, f32 = jnp.bfloat16, jnp.float32
    vmem = pl.BlockSpec(memory_space=pltpu.VMEM)
    anywhere = pl.BlockSpec(memory_space=pl.ANY)
    return pl.pallas_call(
        kernel,
        out_shape=(
            jax.ShapeDtypeStruct(image_query.shape, bf),
            jax.ShapeDtypeStruct(text_query.shape, bf),
        ),
        in_specs=[anywhere] * 3 + [vmem] * 3 + [anywhere] * 2 + [vmem] * 3 + [pl.BlockSpec(memory_space=pltpu.SMEM)],
        out_specs=(vmem, vmem),
        scratch_shapes=[
            pltpu.VMEM(image_query.shape, bf),
            pltpu.VMEM(image_key.shape, bf),
            pltpu.VMEM(image_value.shape, bf),
            pltpu.VMEM((16, BLOCK, HD), bf),
            pltpu.VMEM((16, 2, BLOCK, HD), bf),
            pltpu.VMEM((4, 8, BLOCK, HD), bf),
            pltpu.VMEM((4, TILE, 2 * HD), bf),
            pltpu.VMEM((20, 2, PIECE, HD), bf),
            pltpu.VMEM((4, TILE, HD), f32),
            pltpu.VMEM((4, TILE, 2 * HD), f32),
            pltpu.VMEM((2, TILE, HD), bf),
            pltpu.VMEM((2, 8, HD), f32),
            pltpu.VMEM((2, TILE, HD), bf),
            pltpu.VMEM((2, 8, HD), f32),
            pltpu.VMEM((2, 8, BLOCK, HD), bf),
            pltpu.VMEM((2, TXT, HD), f32),
            pltpu.VMEM((8, 2, 32, HD), f32),
            pltpu.VMEM((32, HD), bf),
            dma((7,)),
            dma((2,)),
            dma((2,)),
            dma((2, 2)),
            dma((2,)),
            dma((2,)),
            dma((2,)),
            dma((2, 2, 2)),
            dma((2,)),
            dma((2,)),
            dma((2,)),
        ],
        compiler_params=pltpu.CompilerParams(
            collective_id=0, has_side_effects=True, vmem_limit_bytes=56 * 2**20
        ),
        name="joint_attention",
    )(
        image_query, image_key, image_value, positions, jnp.asarray(freqs), jnp.asarray(swap, bf),
        stale_key, stale_value, text_query, text_key, text_value, text_len,
    )


def solution(mesh):
    return jax.shard_map(
        body,
        mesh=mesh,
        in_specs=(
            P(("patch", "head"), None),
            P(("patch", "head"), None),
            P(("patch", "head"), None),
            P(None, ("patch", "head")),
            P("patch", "head"),
            P("patch", "head"),
            P(None, "head"),
            P(None, "head"),
            P(None, "head"),
            P(),
        ),
        out_specs=(P(("patch", "head"), None), P(None, "head")),
        check_vma=False,
    )
```

time: 95 us -> 88.5 us (0.932)
  Pallas kernels: 91 us -> 84.5 us
    pallas_call x1, Pallas kernels: 91 us -> 84.5 us  [body(): pl.pallas_call(kernel, out_shape=(jax.ShapeDtypeStruct(image_query.shape,...]
where the time goes in v3:
time: 88.5 us; the launch traced here: 88.3 us
  Pallas kernels  84.5 us (95%)
  local copies, waits for them, and re-layouts  2.58 us (3%)
  between operations  1.3 us (1%)
    pallas_call x1, Pallas kernels, body(): pl.pallas_call(kernel, out_shape=(jax.ShapeDtypeStruct(image_query.shape,...  84.5 us
    unnamed x4, local copies, waits for them, and re-layouts  2.58 us

profile of v3, /device:TPU:1, one launch (start us, length us, event | category | flops | bytes accessed | tf_op | source)
XLA Modules:
  0.0 88.3 jit_solution(3417232385001639426)
XLA Ops:
  1.3 84.5 %joint_attention.1 = (bf16[128,2048]{1,0:T(8,128)(2,1)}, bf16[256,256]{1,0:T(8,128)(2,1)}) custom-call(bf16[128,2048]{1,0:T(8,128)(2,1)} %q_in.1, bf16[128,2048]{1,0:T(8,128)(2,1)} %k_in.1, bf16[128,2048]{1,0:T(8,128)(2,1)} %v_in.1, s32[3,128]{1,0:T(4,128)} %pos_ref.1, bf16[16,128]{1,0:T(8,128)(2,1)} %constant.4.clone.freq_ref, ...), custom_call_target="tpu_custom_call" | custom-call | tf_op jit(solution)/shard_map/joint_attention/pallas_call | solution.py:398
  85.8 0.0 copy-start
  85.8 1.9 %copy.17 = bf16[128,2048]{1,0:T(8,128)(2,1)} copy(bf16[128,2048]{1,0:T(8,128)(2,1)} %get-tuple-element.4) | data formatting | bytes 1048576
  87.7 0.0 copy-done
  87.7 0.7 copy.18
Async XLA Ops:
  85.8 1.9 %copy-start = (bf16[256,256]{1,0:T(8,128)(2,1)S(1)}, bf16[256,256]{1,0:T(8,128)(2,1)}, u32[]{:S(2)}) copy-start(bf16[256,256]{1,0:T(8,128)(2,1)} %get-tuple-element.5) | copy-start | bytes 393220

commit v4 on v3

--- a/solution.py
+++ b/solution.py
@@ -21,12 +21,10 @@
 NEAR_A, NEAR_B, FAR, OWN = (4, 6, 8, 10), (5, 7, 9, 11), (12, 13, 14, 15), (0, 1, 2, 3)
 ITEMS = [
     (0, NEAR_A), (1, NEAR_A),
-    (2, OWN), (3, OWN),
-    (2, NEAR_A), (3, NEAR_A),
-    (2, NEAR_B), (3, NEAR_B),
-    (2, FAR), (3, FAR),
-    (0, NEAR_B), (0, FAR),
-    (1, NEAR_B), (1, FAR),
+    (0, NEAR_B),
+    (2, OWN), (2, NEAR_A), (2, NEAR_B), (2, FAR),
+    (3, OWN), (3, NEAR_A), (3, NEAR_B), (3, FAR),
+    (0, FAR), (1, NEAR_B),
 ]
 ORDER16 = [1, 9, 2, 10, 3, 11, 4, 12, 5, 13, 6, 14, 7, 15, 8]
 ORDER8 = [4, 1, 5, 2, 6, 3, 7, 0]
@@ -155,7 +153,7 @@
 
     def q_copy(d):
         to = (me + d) % 16
-        return remote(qh.at[to], qb.at[c, h], q_sem, (), (x * 4 + y * 2 + to % 2, to // 2))
+        return remote(qh.at[to], qb.at[c, h], q_sem, (c,), (x * 4 + y * 2 + to % 2, to // 2))
 
     def fresh_at(core, head):
         return kv.at[16 + 2 * core + head // 4, :, pl.ds(pl.multiple_of((head % 4) * BLOCK, BLOCK), BLOCK), :]
@@ -183,14 +181,19 @@
     for load in loads[3:]:
         load.wait()
     pl.semaphore_wait(barrier, 30)
-    for d in ORDER16:
-        q_copy(d).start()
-    near_each(0, lambda *a: near(*a).start())
+
+    def send_queries():
+        for d in ORDER16:
+            q_copy(d).start()
+
+    pl.when(c == 0)(send_queries)
     for half in range(2):
         for part in range(2):
             across(half, part).start()
+    pl.when(c == 1)(send_queries)
     for d in ORDER16:
         kv_copy(d).start()
+    near_each(0, lambda *a: near(*a).start())
     near_each(1, lambda *a: near(*a).start())
 
     qb[c, h] = qh[me]
@@ -209,10 +212,6 @@
     def y_copy(t):
         return remote(qb.at[t], qb.at[2 + t], y_sem, (), at(x, 1 - y, c))
 
-    whole(qh.at[pl.ds(0, 15)], q_sem).wait_recv()
-    for t in range(2):
-        y_copy(t).start()
-    loop(0, 2, ready)
 
     def far(half, core, part):
         src = kv.at[4 + 4 * part + 2 * core + half, part]
@@ -227,10 +226,10 @@
 
     valid = lax.broadcasted_iota(jnp.int32, (1, TXT), 1) < len_ref[0]
 
-    def attend(t, ids, text=False):
-        qq = qq_s[t]
-        m = jnp.max(m_s[t], axis=1, keepdims=True)
-        a = acc_s[t]
+    def attend(t, ids, text=False, rows=pl.ds(0, TILE)):
+        qq = qq_s[t, rows]
+        m = jnp.max(m_s[t, rows], axis=1, keepdims=True)
+        a = acc_s[t, rows]
         keys = [lambda n=n: scores(qq, kv[ids[n], 0]) for n in range(len(ids))]
         values = [lambda n=n: kv[ids[n], 1] for n in range(len(ids))]
         if text:
@@ -241,8 +240,8 @@
             following = keys[n + 1]() if n + 1 < len(keys) else None
             m, a = fold(s, values[n](), m, a)
             s = following
-        m_s[t] = jnp.broadcast_to(m, (TILE, HD))
-        acc_s[t] = a
+        m_s[t, rows] = jnp.broadcast_to(m, (a.shape[0], HD))
+        acc_s[t, rows] = a
 
     def text_copy(d):
         to = (rank + d) % 8
@@ -269,6 +268,9 @@
         dst = tout_ref.at[pl.ds(pl.multiple_of(rank * 32, 32), 32), lanes]
         return remote(t_stage, dst, tg_sem, (), (to, h))
 
+    def text_own():
+        return pltpu.make_async_copy(t_stage, tout_ref.at[pl.ds(pl.multiple_of(rank * 32, 32), 32), lanes], in_sem.at[8])
+
     def text_merge():
         whole(t_recv.at[pl.ds(0, 7)], t_sem).wait_recv()
         top = t_recv[0, 1]
@@ -283,7 +285,7 @@
         done = (mixed / total).astype(jnp.bfloat16)
         t_stage[...] = done
         loop(1, 16, lambda d: gather_copy(d).start())
-        tout_ref[pl.ds(pl.multiple_of(rank * 32, 32), 32), lanes] = done
+        text_own().start()
 
     eye = lax.broadcasted_iota(jnp.int32, (HD, HD), 0) == lax.broadcasted_iota(jnp.int32, (HD, HD), 1)
 
@@ -304,35 +306,31 @@
         o_copy(t - 2).start()
         l_copy(t - 2).start()
 
-    def out_copy(t, d):
-        to = (h + d) % 8
-        cols = pl.ds(pl.multiple_of(me * HD, HD), HD)
-        return remote(out_stage.at[t, to], out_ref.at[:, cols], out_sem, (), (x * 4 + y * 2 + t, to))
-
-    def take(t):
-        o_copy(t).wait_recv()
-        l_copy(t).wait_recv()
-        own = jnp.where(t == c, 0, 1)
-        for d in ORDER8:
-            b = (h + d) % 8
-            rows = pl.ds(pl.multiple_of(b * HD, HD), HD)
-            total = acc_s[t, rows, HD:]
-            level = m_s[t, rows] + jnp.log2(total)
-            lev = jnp.sum(jnp.where(eye, l_recv[t, pl.ds(b, 1)], 0.0), axis=1, keepdims=True)
-            top = jnp.maximum(level, lev)
-            wa, wb = jnp.exp2(level - top), jnp.exp2(lev - top)
-            mixed = acc_s[t, rows, :HD] * (wa / total) + o_recv[t, rows].astype(jnp.float32) * wb
-            out_stage[t, b] = (mixed / (wa + wb)).astype(jnp.bfloat16)
-            if d != 0:
-                out_copy(t, d).start()
-
-        @pl.when(own != 0)
-        def _():
-            out_copy(t, 0).start()
-
-        @pl.when(own == 0)
-        def _():
-            out_ref[:, pl.ds(pl.multiple_of(me * HD, HD), HD)] = out_stage[t, h]
+    mine = pl.ds(pl.multiple_of(me * HD, HD), HD)
+
+    def out_copy(t, b):
+        return remote(out_stage.at[t, b], out_ref.at[:, mine], out_sem, (), (x * 4 + y * 2 + t, b))
+
+    def own_copy():
+        return pltpu.make_async_copy(out_stage.at[c, h], out_ref.at[:, mine], in_sem.at[7])
+
+    def take(t, b):
+        rows = pl.ds(pl.multiple_of(b * HD, HD), HD)
+        total = acc_s[t, rows, HD:]
+        level = m_s[t, rows] + jnp.log2(total)
+        lev = jnp.sum(jnp.where(eye, l_recv[t, pl.ds(b, 1)], 0.0), axis=1, keepdims=True)
+        top = jnp.maximum(level, lev)
+        wa, wb = jnp.exp2(level - top), jnp.exp2(lev - top)
+        mixed = acc_s[t, rows, :HD] * (wa / total) + o_recv[t, rows].astype(jnp.float32) * wb
+        out_stage[t, b] = (mixed / (wa + wb)).astype(jnp.bfloat16)
+
+        @pl.when((t != c) | (b != h))
+        def _():
+            out_copy(t, b).start()
+
+        @pl.when((t == c) & (b == h))
+        def _():
+            own_copy().start()
 
     def item(i):
         @pl.when(i == 0)
@@ -345,36 +343,65 @@
             loop(0, 2, lambda t: attend(t, (16 + 2 * t, 17 + 2 * t)))
             near_ready(1)
             text_queries()
+
+        @pl.when(i == 3)
+        def _():
             whole(qb.at[pl.ds(2, 2)], y_sem).wait_recv()
             loop(2, 4, ready)
 
-        @pl.when(i == 5)
+        @pl.when(i == 6)
         def _():
             text_merge()
-
-        @pl.when(i == 8)
-        def _():
             whole(kv.at[pl.ds(12, 4)], far_sem).wait_recv()
 
         t = pick(i, [q for q, _ in ITEMS])
         ids = [pick(i, [pieces[n] for _, pieces in ITEMS]) for n in range(4)]
         attend(t, ids)
 
-        @pl.when((i >= 8) & (i < 10))
+        @pl.when((i == 6) | (i == 10))
         def _():
             give(t)
 
-        @pl.when((i == 11) | (i == 13))
-        def _():
-            take(t)
+        @pl.when(i == 11)
+        def _():
+            o_copy(0).wait_recv()
+            l_copy(0).wait_recv()
+            for d in ORDER8:
+                take(0, (h + d) % 8)
+
+    def begin(t):
+        @pl.when(t == c)
+        def _():
+            whole(qh.at[pl.ds(0, 7)], q_sem, (t,)).wait_recv()
+
+        @pl.when(t != c)
+        def _():
+            whole(qh.at[pl.ds(0, 8)], q_sem, (t,)).wait_recv()
+
+        y_copy(t).start()
+        ready(t)
+        attend(t, (2 - 2 * t, 3 - 2 * t), text=True)
+
+    def finish(half):
+        side = (h // 4 + 1 + half) % 2
+        attend(1, FAR, rows=pl.ds(pl.multiple_of(side * PIECE, PIECE), PIECE))
+
+        @pl.when(half == 0)
+        def _():
+            o_copy(1).wait_recv()
+            l_copy(1).wait_recv()
+
+        for d in (1, 2, 3, 0):
+            take(1, side * 4 + (h + d) % 4)
 
     whole(kv.at[pl.ds(0, 2)], core_sem).wait_recv()
-    loop(0, 2, lambda t: attend(t, (2 - 2 * t, 3 - 2 * t), text=True))
-    loop(0, 14, item)
+    loop(0, 2, begin)
+    loop(0, 13, item)
+    loop(0, 2, finish)
 
     for half in range(2):
         whole(kv.at[pl.ds(4, 4)], near_sem, (half,)).wait_send()
-    whole(qh.at[pl.ds(0, 15)], q_sem).wait_send()
+    whole(qh.at[pl.ds(0, 15)], q_sem, (c,)).wait_send()
     whole(kvh.at[pl.ds(0, 15)], kv_sem).wait_send()
     whole(kv.at[pl.ds(0, 2)], core_sem).wait_send()
     whole(kv.at[pl.ds(12, 4)], far_sem).wait_send()
@@ -385,6 +412,8 @@
     whole(t_recv.at[pl.ds(0, 7)], t_sem).wait_send()
     whole(qh.at[pl.ds(0, 15), pl.ds(0, 32)], tg_sem).wait_send()
     whole(qh.at[pl.ds(0, 15), pl.ds(0, 32)], tg_sem).wait_recv()
+    text_own().wait()
+    own_copy().wait()
     whole(qh.at[pl.ds(0, 15)], out_sem).wait_send()
     whole(qh.at[pl.ds(0, 15)], out_sem).wait_recv()
 
@@ -402,7 +431,7 @@
             jax.ShapeDtypeStruct(text_query.shape, bf),
         ),
         in_specs=[anywhere] * 3 + [vmem] * 3 + [anywhere] * 2 + [vmem] * 3 + [pl.BlockSpec(memory_space=pltpu.SMEM)],
-        out_specs=(vmem, vmem),
+        out_specs=(anywhere, anywhere),
         scratch_shapes=[
             pltpu.VMEM(image_query.shape, bf),
             pltpu.VMEM(image_key.shape, bf),
@@ -422,8 +451,8 @@
             pltpu.VMEM((2, TXT, HD), f32),
             pltpu.VMEM((8, 2, 32, HD), f32),
             pltpu.VMEM((32, HD), bf),
-            dma((7,)),
-            dma((2,)),
+            dma((9,)),
+            dma((2, 2)),
             dma((2,)),
             dma((2, 2)),
             dma((2,)),

time: 88.5 us -> 85.3 us (0.964)
  Pallas kernels: 84.5 us -> 81.2 us
    pallas_call x1, Pallas kernels: 84.5 us -> 81.2 us  [body(): pl.pallas_call(kernel, out_shape=(jax.ShapeDtypeStruct(image_query.shape,...]
where the time goes in v4:
time: 85.3 us; the launch traced here: 85.1 us
  Pallas kernels  81.2 us (95%)
  local copies, waits for them, and re-layouts  2.58 us (3%)
  between operations  1.3 us (2%)
    pallas_call x1, Pallas kernels, body(): pl.pallas_call(kernel, out_shape=(jax.ShapeDtypeStruct(image_query.shape,...  81.2 us
    unnamed x4, local copies, waits for them, and re-layouts  2.58 us

profile of v4, /device:TPU:1, one launch (start us, length us, event | category | flops | bytes accessed | tf_op | source)
XLA Modules:
  0.0 85.1 jit_solution(4730171600234923119)
XLA Ops:
  1.3 81.2 %joint_attention.1 = (bf16[128,2048]{1,0:T(8,128)(2,1)}, bf16[256,256]{1,0:T(8,128)(2,1)}) custom-call(bf16[128,2048]{1,0:T(8,128)(2,1)} %q_in.1, bf16[128,2048]{1,0:T(8,128)(2,1)} %k_in.1, bf16[128,2048]{1,0:T(8,128)(2,1)} %v_in.1, s32[3,128]{1,0:T(4,128)} %pos_ref.1, bf16[16,128]{1,0:T(8,128)(2,1)} %constant.4.clone.freq_ref, ...), custom_call_target="tpu_custom_call" | custom-call | tf_op jit(solution)/shard_map/joint_attention/pallas_call | solution.py:427
  82.5 0.0 copy-start
  82.5 1.9 %copy.17 = bf16[128,2048]{1,0:T(8,128)(2,1)} copy(bf16[128,2048]{1,0:T(8,128)(2,1)} %get-tuple-element.4) | data formatting | bytes 1048576
  84.4 0.0 copy-done
  84.4 0.7 copy.18
Async XLA Ops:
  82.5 1.9 %copy-start = (bf16[256,256]{1,0:T(8,128)(2,1)S(1)}, bf16[256,256]{1,0:T(8,128)(2,1)}, u32[]{:S(2)}) copy-start(bf16[256,256]{1,0:T(8,128)(2,1)} %get-tuple-element.5) | copy-start | bytes 393220
